TPU v7x, 256 devices: a whole 4x4x8 slice. The times are simulated.
256 devices in a mesh: rcv: 16 (over z_hi, x), tf: 16 (over y, z_lo, core).
Axes of the slice: x: 4, y: 4, z: 8 (z_hi: 4, z_lo: 2; z = z_hi * 2 + z_lo), core: 2. Of those that a mesh axis runs over, the one named last changes fastest.
Arguments:
- observed: bfloat16 [2, 16384, 4096], P(None, 'rcv', 'tf'), may hold values from -200 to 200
- synthetic: bfloat16 [2, 16384, 4096], P(None, 'rcv', 'tf'), may hold values from -100 to 100
- live: int32 [2, 16384], P(None, 'rcv'), may hold values 0 or 1
- bins: int32 [1024], replicated, may hold values from 1 to 2047
Outputs:
- adjoint: bfloat16 [2, 16384, 4096], P(None, 'rcv', 'tf')
All inputs are finite; a program needn't handle non-finite values. No bound on the sum of `live` on one device may be relied on, other than what follows from the above.
Results may differ from a plain program's by a relative error of at most 0.0041.
The roundings to bfloat16 on the way count: a program that leaves them out, or rounds other values in their place, can miss the bound.
Values may be sent and summed in bfloat16 or wider, within the bound.
A program may use at most 128 MiB of HBM per device.

v0:
```python
import math

import jax
import jax.numpy as jnp
from jax import lax
from jax.sharding import PartitionSpec as P

NT = 4096


def make_tables(start, count, bins):
    times = start + jnp.arange(count, dtype=jnp.int32)
    angle = (times[:, None] * bins[None, :] % NT).astype(jnp.float32) * (2.0 * math.pi / NT)
    scale = NT ** (-0.5)
    return (
        (jnp.cos(angle) * scale).astype(jnp.bfloat16),
        (-jnp.sin(angle) * scale).astype(jnp.bfloat16),
    )


def local_sums(spec, weight):
    obs_re, obs_im, syn_re, syn_im = spec
    cross_re = jnp.sum(weight * (syn_re * obs_re + syn_im * obs_im), axis=-2)
    cross_im = jnp.sum(weight * (syn_re * obs_im - syn_im * obs_re), axis=-2)
    power = jnp.sum(weight * (syn_re * syn_re + syn_im * syn_im), axis=-2)
    return (cross_re, cross_im, power)


def correct(totals, spec, weight):
    cross_re, cross_im, power = totals
    obs_re, obs_im, syn_re, syn_im = spec
    denom = power + 0.001 * jnp.max(power, axis=-1, keepdims=True)
    w_re = (cross_re / denom)[..., None, :]
    w_im = (cross_im / denom)[..., None, :]
    res_re = (weight * (w_re * syn_re - w_im * syn_im - obs_re)).astype(jnp.bfloat16)
    res_im = (weight * (w_re * syn_im + w_im * syn_re - obs_im)).astype(jnp.bfloat16)
    return (res_re, res_im)


def on_device(observed, synthetic, live, bins):
    shots = observed.shape[0]
    r_dev = observed.shape[1]
    t_loc = observed.shape[2]
    n_tf = lax.axis_size("tf")
    n_freq = bins.shape[0]
    livef = live.astype(jnp.float32)
    last = (((1,), (1,)), ((), ()))
    r_sub = r_dev // n_tf
    n_time = t_loc * n_tf
    span = math.gcd(n_time, 512)
    n_blocks = n_time // span
    weight = lax.dynamic_slice_in_dim(livef, lax.axis_index("tf") * r_sub, r_sub, 1)
    stacked = jnp.stack([observed, synthetic])
    traces = lax.all_to_all(stacked, "tf", split_axis=2, concat_axis=3, tiled=True)
    flat = traces.reshape(2 * shots * r_sub, n_time)

    def forward_block(carry, step):
        cos_tab, sin_tab = make_tables(step * span, span, bins)
        block = lax.dynamic_slice_in_dim(flat, step * span, span, 1)
        return (
            (
                carry[0] + jnp.dot(block, cos_tab, preferred_element_type=jnp.float32),
                carry[1] + jnp.dot(block, sin_tab, preferred_element_type=jnp.float32),
            ),
            None,
        )

    empty = jnp.zeros((flat.shape[0], n_freq), jnp.float32)
    (spec_re, spec_im), _ = lax.scan(
        forward_block, (empty, empty), jnp.arange(n_blocks, dtype=jnp.int32)
    )
    spec_re, spec_im = (spec_re, spec_im)
    spec_re = spec_re.reshape(2, shots, r_sub, n_freq)
    spec_im = spec_im.reshape(2, shots, r_sub, n_freq)
    spec = (spec_re[0], spec_im[0], spec_re[1], spec_im[1])
    weight_rows = weight[:, :, None]
    cross_re, cross_im, power = local_sums(spec, weight_rows)
    totals = lax.psum((cross_re, cross_im, power), ("rcv", "tf"))
    res_re, res_im = correct(totals, spec, weight_rows)
    inverse_res_re = res_re.reshape(shots * r_sub, n_freq)
    inverse_res_im = res_im.reshape(shots * r_sub, n_freq)

    def inverse_block(carry, step):
        cos_tab, sin_tab = make_tables(step * span, span, bins)
        part = lax.dot_general(inverse_res_re, cos_tab, last, preferred_element_type=jnp.float32)
        part = part + lax.dot_general(
            inverse_res_im, sin_tab, last, preferred_element_type=jnp.float32
        )
        return (carry, (2.0 * part).astype(jnp.bfloat16))

    _, blocks = lax.scan(inverse_block, jnp.int32(0), jnp.arange(n_blocks, dtype=jnp.int32))
    whole = jnp.moveaxis(blocks, 0, 1).reshape(inverse_res_re.shape[0], n_time)
    whole = whole.reshape(shots, r_sub, n_time)
    return lax.all_to_all(whole, "tf", split_axis=2, concat_axis=1, tiled=True)


def solution(mesh):
    in_specs = (P(None, "rcv", "tf"), P(None, "rcv", "tf"), P(None, "rcv"), P())
    out_specs = P(None, "rcv", "tf")
    return jax.shard_map(
        on_device, mesh=mesh, in_specs=in_specs, out_specs=out_specs, check_vma=False
    )
```

profile of v0, /device:TPU:1, one launch (start us, length us, event | category | flops | bytes accessed | tf_op | source)
XLA Modules:
  0.0 460.8 jit_solution(14352297473412699331)
XLA Ops:
  16.8 26.2 %all-to-all-done = bf16[2,2,1024,256]{3,1,0,2:T(2,128)(2,1)S(1)} async-done(((bf16[2,2,1024,256]{3,1,0,2:T(2,128)(2,1)}), bf16[2,2,1024,256]{3,1,0,2:T(2,128)(2,1)S(1)}, u32[]{:S(2)}, u32[]{:S(2)}) %all-to-all-start) | async-done | bytes 2097184 | tf_op jit(solution)/shard_map/all_to_all | solution.py:54
  46.5 155.5 %while.28 = (s32[]{:T(128)}, f32[256,1024]{1,0:T(8,128)S(1)}, f32[256,1024]{1,0:T(8,128)S(1)}, s32[8]{0:T(128)S(1)}, bf16[256,4096]{1,0:T(8,128)(2,1)}, /*index=...) while((s32[]{:T(128)}, f32[256,1024]{1,0:T(8,128)S(1)}, ...), condition=%wide.region_1.2_spmd.clone, body=%wide.region_0.1_spmd.clone.sunk | while | flops 555221504 | bytes 4733110 | solution.py:69
  47.9 9.1 %convolution_add_fusion.6 = f32[256,1024]{1,0:T(8,128)S(1)} fusion(f32[256,1024]{1,0:T(8,128)S(1)} %get-tuple-element.311, s32[1024]{0:T(1024)S(1)} %get-tuple-element.324, s32[512]{0:T(512)S(1)} %iota_add_fusion.5, pred[]{:T(512)S(6)} %compare.5, bf16[256,4096]{1,0:T(8,128)(2,1)} %get-tuple-element.323, s32[]{:T(128)S(6)} %select_n.64), kind=kOutput, calls=%fused_computation.39.clone.1 | convolution fusion | flops 277872640 | bytes 2365445 | tf_op jit(solution)/shard_map/while/body/eval_jaxpr/dot_general | solution.py:63
  57.0 9.0 %convolution_add_fusion.5 = f32[256,1024]{1,0:T(8,128)S(1)} fusion(f32[256,1024]{1,0:T(8,128)S(1)} %get-tuple-element.310, s32[1024]{0:T(1024)S(1)} %get-tuple-element.324, s32[512]{0:T(512)S(1)} %iota_add_fusion.5, pred[]{:T(512)S(6)} %compare.5, bf16[256,4096]{1,0:T(8,128)(2,1)} %get-tuple-element.323, s32[]{:T(128)S(6)} %select_n.64), kind=kOutput, calls=%fused_computation.40.clone.1 | convolution fusion | flops 277348352 | bytes 2365445 | tf_op jit(solution)/shard_map/while/body/eval_jaxpr/dot_general | solution.py:62
  67.3 9.1 %convolution_add_fusion.6 = f32[256,1024]{1,0:T(8,128)S(1)} fusion(f32[256,1024]{1,0:T(8,128)S(1)} %get-tuple-element.311, s32[1024]{0:T(1024)S(1)} %get-tuple-element.324, s32[512]{0:T(512)S(1)} %iota_add_fusion.5, pred[]{:T(512)S(6)} %compare.5, bf16[256,4096]{1,0:T(8,128)(2,1)} %get-tuple-element.323, s32[]{:T(128)S(6)} %select_n.64), kind=kOutput, calls=%fused_computation.39.clone.1 | convolution fusion | flops 277872640 | bytes 2365445 | tf_op jit(solution)/shard_map/while/body/eval_jaxpr/dot_general | solution.py:63
  76.4 9.0 %convolution_add_fusion.5 = f32[256,1024]{1,0:T(8,128)S(1)} fusion(f32[256,1024]{1,0:T(8,128)S(1)} %get-tuple-element.310, s32[1024]{0:T(1024)S(1)} %get-tuple-element.324, s32[512]{0:T(512)S(1)} %iota_add_fusion.5, pred[]{:T(512)S(6)} %compare.5, bf16[256,4096]{1,0:T(8,128)(2,1)} %get-tuple-element.323, s32[]{:T(128)S(6)} %select_n.64), kind=kOutput, calls=%fused_computation.40.clone.1 | convolution fusion | flops 277348352 | bytes 2365445 | tf_op jit(solution)/shard_map/while/body/eval_jaxpr/dot_general | solution.py:62
  86.7 9.1 %convolution_add_fusion.6 = f32[256,1024]{1,0:T(8,128)S(1)} fusion(f32[256,1024]{1,0:T(8,128)S(1)} %get-tuple-element.311, s32[1024]{0:T(1024)S(1)} %get-tuple-element.324, s32[512]{0:T(512)S(1)} %iota_add_fusion.5, pred[]{:T(512)S(6)} %compare.5, bf16[256,4096]{1,0:T(8,128)(2,1)} %get-tuple-element.323, s32[]{:T(128)S(6)} %select_n.64), kind=kOutput, calls=%fused_computation.39.clone.1 | convolution fusion | flops 277872640 | bytes 2365445 | tf_op jit(solution)/shard_map/while/body/eval_jaxpr/dot_general | solution.py:63
  95.8 9.0 %convolution_add_fusion.5 = f32[256,1024]{1,0:T(8,128)S(1)} fusion(f32[256,1024]{1,0:T(8,128)S(1)} %get-tuple-element.310, s32[1024]{0:T(1024)S(1)} %get-tuple-element.324, s32[512]{0:T(512)S(1)} %iota_add_fusion.5, pred[]{:T(512)S(6)} %compare.5, bf16[256,4096]{1,0:T(8,128)(2,1)} %get-tuple-element.323, s32[]{:T(128)S(6)} %select_n.64), kind=kOutput, calls=%fused_computation.40.clone.1 | convolution fusion | flops 277348352 | bytes 2365445 | tf_op jit(solution)/shard_map/while/body/eval_jaxpr/dot_general | solution.py:62
  106.1 9.1 %convolution_add_fusion.6 = f32[256,1024]{1,0:T(8,128)S(1)} fusion(f32[256,1024]{1,0:T(8,128)S(1)} %get-tuple-element.311, s32[1024]{0:T(1024)S(1)} %get-tuple-element.324, s32[512]{0:T(512)S(1)} %iota_add_fusion.5, pred[]{:T(512)S(6)} %compare.5, bf16[256,4096]{1,0:T(8,128)(2,1)} %get-tuple-element.323, s32[]{:T(128)S(6)} %select_n.64), kind=kOutput, calls=%fused_computation.39.clone.1 | convolution fusion | flops 277872640 | bytes 2365445 | tf_op jit(solution)/shard_map/while/body/eval_jaxpr/dot_general | solution.py:63
  115.2 9.0 %convolution_add_fusion.5 = f32[256,1024]{1,0:T(8,128)S(1)} fusion(f32[256,1024]{1,0:T(8,128)S(1)} %get-tuple-element.310, s32[1024]{0:T(1024)S(1)} %get-tuple-element.324, s32[512]{0:T(512)S(1)} %iota_add_fusion.5, pred[]{:T(512)S(6)} %compare.5, bf16[256,4096]{1,0:T(8,128)(2,1)} %get-tuple-element.323, s32[]{:T(128)S(6)} %select_n.64), kind=kOutput, calls=%fused_computation.40.clone.1 | convolution fusion | flops 277348352 | bytes 2365445 | tf_op jit(solution)/shard_map/while/body/eval_jaxpr/dot_general | solution.py:62
  125.5 9.1 %convolution_add_fusion.6 = f32[256,1024]{1,0:T(8,128)S(1)} fusion(f32[256,1024]{1,0:T(8,128)S(1)} %get-tuple-element.311, s32[1024]{0:T(1024)S(1)} %get-tuple-element.324, s32[512]{0:T(512)S(1)} %iota_add_fusion.5, pred[]{:T(512)S(6)} %compare.5, bf16[256,4096]{1,0:T(8,128)(2,1)} %get-tuple-element.323, s32[]{:T(128)S(6)} %select_n.64), kind=kOutput, calls=%fused_computation.39.clone.1 | convolution fusion | flops 277872640 | bytes 2365445 | tf_op jit(solution)/shard_map/while/body/eval_jaxpr/dot_general | solution.py:63
  134.6 9.0 %convolution_add_fusion.5 = f32[256,1024]{1,0:T(8,128)S(1)} fusion(f32[256,1024]{1,0:T(8,128)S(1)} %get-tuple-element.310, s32[1024]{0:T(1024)S(1)} %get-tuple-element.324, s32[512]{0:T(512)S(1)} %iota_add_fusion.5, pred[]{:T(512)S(6)} %compare.5, bf16[256,4096]{1,0:T(8,128)(2,1)} %get-tuple-element.323, s32[]{:T(128)S(6)} %select_n.64), kind=kOutput, calls=%fused_computation.40.clone.1 | convolution fusion | flops 277348352 | bytes 2365445 | tf_op jit(solution)/shard_map/while/body/eval_jaxpr/dot_general | solution.py:62
  144.9 9.1 %convolution_add_fusion.6 = f32[256,1024]{1,0:T(8,128)S(1)} fusion(f32[256,1024]{1,0:T(8,128)S(1)} %get-tuple-element.311, s32[1024]{0:T(1024)S(1)} %get-tuple-element.324, s32[512]{0:T(512)S(1)} %iota_add_fusion.5, pred[]{:T(512)S(6)} %compare.5, bf16[256,4096]{1,0:T(8,128)(2,1)} %get-tuple-element.323, s32[]{:T(128)S(6)} %select_n.64), kind=kOutput, calls=%fused_computation.39.clone.1 | convolution fusion | flops 277872640 | bytes 2365445 | tf_op jit(solution)/shard_map/while/body/eval_jaxpr/dot_general | solution.py:63
  154.0 9.0 %convolution_add_fusion.5 = f32[256,1024]{1,0:T(8,128)S(1)} fusion(f32[256,1024]{1,0:T(8,128)S(1)} %get-tuple-element.310, s32[1024]{0:T(1024)S(1)} %get-tuple-element.324, s32[512]{0:T(512)S(1)} %iota_add_fusion.5, pred[]{:T(512)S(6)} %compare.5, bf16[256,4096]{1,0:T(8,128)(2,1)} %get-tuple-element.323, s32[]{:T(128)S(6)} %select_n.64), kind=kOutput, calls=%fused_computation.40.clone.1 | convolution fusion | flops 277348352 | bytes 2365445 | tf_op jit(solution)/shard_map/while/body/eval_jaxpr/dot_general | solution.py:62
  164.3 9.1 %convolution_add_fusion.6 = f32[256,1024]{1,0:T(8,128)S(1)} fusion(f32[256,1024]{1,0:T(8,128)S(1)} %get-tuple-element.311, s32[1024]{0:T(1024)S(1)} %get-tuple-element.324, s32[512]{0:T(512)S(1)} %iota_add_fusion.5, pred[]{:T(512)S(6)} %compare.5, bf16[256,4096]{1,0:T(8,128)(2,1)} %get-tuple-element.323, s32[]{:T(128)S(6)} %select_n.64), kind=kOutput, calls=%fused_computation.39.clone.1 | convolution fusion | flops 277872640 | bytes 2365445 | tf_op jit(solution)/shard_map/while/body/eval_jaxpr/dot_general | solution.py:63
  173.4 9.0 %convolution_add_fusion.5 = f32[256,1024]{1,0:T(8,128)S(1)} fusion(f32[256,1024]{1,0:T(8,128)S(1)} %get-tuple-element.310, s32[1024]{0:T(1024)S(1)} %get-tuple-element.324, s32[512]{0:T(512)S(1)} %iota_add_fusion.5, pred[]{:T(512)S(6)} %compare.5, bf16[256,4096]{1,0:T(8,128)(2,1)} %get-tuple-element.323, s32[]{:T(128)S(6)} %select_n.64), kind=kOutput, calls=%fused_computation.40.clone.1 | convolution fusion | flops 277348352 | bytes 2365445 | tf_op jit(solution)/shard_map/while/body/eval_jaxpr/dot_general | solution.py:62
  183.6 9.1 %convolution_add_fusion.6 = f32[256,1024]{1,0:T(8,128)S(1)} fusion(f32[256,1024]{1,0:T(8,128)S(1)} %get-tuple-element.311, s32[1024]{0:T(1024)S(1)} %get-tuple-element.324, s32[512]{0:T(512)S(1)} %iota_add_fusion.5, pred[]{:T(512)S(6)} %compare.5, bf16[256,4096]{1,0:T(8,128)(2,1)} %get-tuple-element.323, s32[]{:T(128)S(6)} %select_n.64), kind=kOutput, calls=%fused_computation.39.clone.1 | convolution fusion | flops 277872640 | bytes 2365445 | tf_op jit(solution)/shard_map/while/body/eval_jaxpr/dot_general | solution.py:63
  192.8 9.0 %convolution_add_fusion.5 = f32[256,1024]{1,0:T(8,128)S(1)} fusion(f32[256,1024]{1,0:T(8,128)S(1)} %get-tuple-element.310, s32[1024]{0:T(1024)S(1)} %get-tuple-element.324, s32[512]{0:T(512)S(1)} %iota_add_fusion.5, pred[]{:T(512)S(6)} %compare.5, bf16[256,4096]{1,0:T(8,128)(2,1)} %get-tuple-element.323, s32[]{:T(128)S(6)} %select_n.64), kind=kOutput, calls=%fused_computation.40.clone.1 | convolution fusion | flops 277348352 | bytes 2365445 | tf_op jit(solution)/shard_map/while/body/eval_jaxpr/dot_general | solution.py:62
  202.5 77.9 %all-reduce = (f32[2,1024]{1,0:T(2,128)S(1)}, f32[2,1024]{1,0:T(2,128)S(1)}, f32[2,1024]{1,0:T(2,128)S(1)}) all-reduce(f32[2,1024]{1,0:T(2,128)S(1)} %get-tuple-element.188, f32[2,1024]{1,0:T(2,128)S(1)} %get-tuple-element.187, f32[2,1024]{1,0:T(2,128)S(1)} %get-tuple-element.186), channel_id=1, replica_groups=mesh['rcv'=16,'tf'=16] {'rcv','tf'}, use_global_device_ids=true, to_apply=%region_8.9 | all-reduce | flops 6144 | bytes 49152 | tf_op jit(solution)/shard_map/psum | solution.py:78
  280.9 145.4 %while.27 = (s32[]{:T(128)}, bf16[8,128,512]{1,2,0:T(8,128)(2,1)}, s32[8]{0:T(128)S(1)}, s32[1024]{0:T(1024)S(1)}, bf16[128,1024]{1,0:T(8,128)(2,1)S(1)}, /*inde...) while((s32[]{:T(128)}, bf16[8,128,512]{1,2,0:T(8,128)(2,1)}, s32[8]{0:T(128)S(1)}, ...), condition=%wide.region_10.11_spmd, body=%wide.region_9.10_spmd.sunk | while | flops 285934080 | bytes 1194609 | solution.py:91
  290.2 8.8 %fusion.60 = bf16[8,128,512]{1,2,0:T(8,128)(2,1)} fusion(bf16[8,128,512]{1,2,0:T(8,128)(2,1)} %get-tuple-element.338, s32[]{:T(128)} %get-tuple-element.337, f32[512,128]{1,0:T(8,128)S(1)} %fusion.59, bf16[128,1024]{1,0:T(8,128)(2,1)S(1)} %get-tuple-element.350, s32[1024]{0:T(1024)S(1)} %get-tuple-element.348, s32[512]{0:T(512)S(1)} %iota_add_fusion.4), kind=kOutput, calls=%fused_computation.14.clone.1 | convolution fusion | flops 143327232 | bytes 662016 | tf_op jit(solution)/shard_map/while/body/eval_jaxpr/dot_general | solution.py:86
  308.4 8.8 %fusion.60 = bf16[8,128,512]{1,2,0:T(8,128)(2,1)} fusion(bf16[8,128,512]{1,2,0:T(8,128)(2,1)} %get-tuple-element.338, s32[]{:T(128)} %get-tuple-element.337, f32[512,128]{1,0:T(8,128)S(1)} %fusion.59, bf16[128,1024]{1,0:T(8,128)(2,1)S(1)} %get-tuple-element.350, s32[1024]{0:T(1024)S(1)} %get-tuple-element.348, s32[512]{0:T(512)S(1)} %iota_add_fusion.4), kind=kOutput, calls=%fused_computation.14.clone.1 | convolution fusion | flops 143327232 | bytes 662016 | tf_op jit(solution)/shard_map/while/body/eval_jaxpr/dot_general | solution.py:86
  362.8 8.8 %fusion.60 = bf16[8,128,512]{1,2,0:T(8,128)(2,1)} fusion(bf16[8,128,512]{1,2,0:T(8,128)(2,1)} %get-tuple-element.338, s32[]{:T(128)} %get-tuple-element.337, f32[512,128]{1,0:T(8,128)S(1)} %fusion.59, bf16[128,1024]{1,0:T(8,128)(2,1)S(1)} %get-tuple-element.350, s32[1024]{0:T(1024)S(1)} %get-tuple-element.348, s32[512]{0:T(512)S(1)} %iota_add_fusion.4), kind=kOutput, calls=%fused_computation.14.clone.1 | convolution fusion | flops 143327232 | bytes 662016 | tf_op jit(solution)/shard_map/while/body/eval_jaxpr/dot_general | solution.py:86
  431.7 20.1 %all_to_all.33 = bf16[16,2,16384]{2,1,0:T(2,128)(2,1)} all-to-all(bf16[16,2,16384]{2,1,0:T(2,128)(2,1)S(1)} %reshape.55), channel_id=1, replica_groups=mesh['rcv'=16,'tf'=16] {'tf'}, dimensions={0} | all-to-all | bytes 2097152 | tf_op jit(solution)/shard_map/all_to_all | solution.py:94
  (71 shorter events, 152.8 us)
Async XLA Ops:
  8.5 34.5 %all-to-all-start = ((bf16[2,2,1024,256]{3,1,0,2:T(2,128)(2,1)}), bf16[2,2,1024,256]{3,1,0,2:T(2,128)(2,1)S(1)}, u32[]{:S(2)}, u32[]{:S(2)}) async-start(bf16[2,2,1024,256]{3,1,0,2:T(2,128)(2,1)} %pad_maximum_fusion), calls=%async_computation | async-start | bytes 4194304 | tf_op jit(solution)/shard_map/all_to_all | solution.py:54
  44.2 2.3 copy-start
  44.2 2.3 copy-start.1
where the time goes:
time: 467 us; the launch traced here: 461 us
  matrix products  279 us (60%)
  blocking collectives  98 us (21%)
  local copies, waits for them, and re-layouts  31.9 us (7%)
  waiting for transfers between devices  26.2 us (6%)
  loops' own time  11.6 us (2%)
  starting transfers between devices  7.34 us (2%)
  other arithmetic  5.86 us (1%)
    psum x1, blocking collectives, on_device(): totals = lax.psum((cross_re, cross_im, power), ('rcv', 'tf'))  77.9 us
    dot_general x8, matrix products, forward_block(): jnp.dot(block, sin_tab, preferred_element_type=jnp.float32)  72.8 us
    dot_general x8, matrix products, forward_block(): jnp.dot(block, cos_tab, preferred_element_type=jnp.float32)  72.2 us
    dot_general x8, matrix products, inverse_block(): lax.dot_general(inverse_res_im, sin_tab, last, preferred_element_type=jnp...  70.8 us
    dot_general x8, matrix products, inverse_block(): lax.dot_general(inverse_res_re, cos_tab, last, preferred_element_type=jnp...  63.4 us
    all_to_all x1, waiting for transfers between devices, on_device(): lax.all_to_all(stacked, 'tf', split_axis=2, concat_axis=3, tiled=True)  26.2 us
    all_to_all x1, blocking collectives, on_device(): return lax.all_to_all(whole, 'tf', split_axis=2, concat_axis=1, tiled=True)  20.1 us
    dynamic_slice x16, local copies, waits for them, and re-layouts, on_device(): lax.scan(forward_block, (empty, empty), jnp.arange(n_blocks, dtype=jnp.in...  10.1 us
  transfers between devices with their start and end apart: 1, of which 1 were waited for; matrix products, arithmetic and copies ran while one was open for 0% of the time, Pallas kernels for 0%

commit v1 on v0

v1 whole, which is shorter than its diff:
```python
import math

import jax
import jax.numpy as jnp
from jax import lax
from jax.experimental import pallas as pl
from jax.experimental.pallas import tpu as pltpu
from jax.sharding import PartitionSpec as P

NT = 4096
MESH = pl.DeviceIdType.MESH
N_TF = 16
N_Y = 4
N_J = 4
SPAN = NT // N_TF
QUART = NT // N_Y
NF = 1024
SEED = 64
SLOTS = ((2, 0), (2, 1), (2, 2), (2, 3), (3, 0), (1, 0), (3, 1), (1, 1),
         (3, 2), (1, 2), (3, 3), (1, 3), (0, 2), (0, 3), (0, 1))


def cos_sin(turns):
    k = turns & (NT - 1)
    quadrant = (k + NT // 8) // (NT // 4)
    angle = (k - quadrant * (NT // 4)).astype(jnp.float32) * (2.0 * math.pi / NT)
    sq = angle * angle
    s = angle + angle * sq * (-1 / 6 + sq * (1 / 120 + sq * (-1 / 5040 + sq * (1 / 362880))))
    c = 1.0 + sq * (-0.5 + sq * (1 / 24 + sq * (-1 / 720 + sq * (1 / 40320))))
    odd = (quadrant & 1) == 1
    cos = jnp.where(odd, s, c)
    sin = jnp.where(odd, c, s)
    turn = quadrant & 3
    cos = jnp.where((turn == 1) | (turn == 2), -cos, cos)
    sin = jnp.where(turn >= 2, -sin, sin)
    return cos, sin


def peer_of(y, j, dy, dj):
    dz, dc = dj // 2, dj % 2
    z = (j // 2 + dz) % 2
    c = (j + dc) % 2
    return (y + dy) % N_Y, z * 2 + c


def wait_bytes(view, sem):
    pltpu.make_async_copy(view, view, sem).wait()


def kernel(r_sub, n_x, n_zh, bins_ref, live_ref, obs_ref, syn_ref, out_ref,
           xbuf, tab, seed, first, rot, spec, res, outbuf, wrow,
           part, from_tf, sum_tf, from_x, sum_x, from_z, total,
           in_send, in_recv, tf_send, tf_recv, x_send, x_recv, z_send, z_recv, out_send, out_recv):
    me = lax.axis_index("tf")
    mr = lax.axis_index("rcv")
    y = me // N_J
    j = me % N_J
    x = mr % n_x
    zh = mr // n_x
    shots = 2
    rows = 2 * r_sub

    barrier = pltpu.get_barrier_semaphore()
    count = 0
    for dx in range(1, n_x):
        pl.semaphore_signal(barrier, inc=1, device_id={"rcv": zh * n_x + (x + dx) % n_x}, device_id_type=MESH)
        count += 1
    for dz in range(1, n_zh):
        pl.semaphore_signal(barrier, inc=1, device_id={"rcv": ((zh + dz) % n_zh) * n_x + x}, device_id_type=MESH)
        count += 1
    for dy, dj in SLOTS:
        py, pj = peer_of(y, j, dy, dj)
        pl.semaphore_signal(barrier, inc=1, device_id={"tf": py * N_J + pj}, device_id_type=MESH)
        count += 1
    pl.semaphore_wait(barrier, count)

    def landing(s, a):
        row = pl.multiple_of(y * rows + a * r_sub, r_sub)
        return xbuf.at[s, pl.ds(row, r_sub), pl.ds(pl.multiple_of(j * SPAN, SPAN), SPAN)]

    for s in range(shots):
        for dy, dj in SLOTS:
            py, pj = peer_of(y, j, dy, dj)
            peer = py * N_J + pj
            for a, ref in enumerate((obs_ref, syn_ref)):
                pltpu.make_async_remote_copy(
                    src_ref=ref.at[s, pl.ds(pl.multiple_of(peer * r_sub, r_sub), r_sub), :],
                    dst_ref=landing(s, a), send_sem=in_send.at[s], recv_sem=in_recv.at[s],
                    device_id={"tf": peer}, device_id_type=MESH).start()
        for a, ref in enumerate((obs_ref, syn_ref)):
            pltpu.make_async_copy(
                ref.at[s, pl.ds(pl.multiple_of(me * r_sub, r_sub), r_sub), :],
                landing(s, a), in_recv.at[s]).start()

    bins = bins_ref[...]
    times = lax.broadcasted_iota(jnp.int32, (SEED, NF), 0)
    cos, sin = cos_sin(times * bins)
    scale = NT ** (-0.5)
    seed[0] = cos * scale
    seed[1] = sin * scale
    steps = QUART // SEED
    times = lax.broadcasted_iota(jnp.int32, (steps, NF), 0) * SEED
    cos, sin = cos_sin(times * bins)
    first[0] = cos
    first[1] = sin
    turn = bins & 3
    rot[0:1, :] = jnp.where(turn == 0, 1.0, jnp.where(turn == 2, -1.0, 0.0))
    rot[1:2, :] = jnp.where(turn == 1, 1.0, jnp.where(turn == 3, -1.0, 0.0))
    rot[2:3, :] = jnp.where((turn & 1) == 0, 1.0, -1.0)

    def make_rows(i, carry):
        c0 = first[0, pl.ds(i, 1), :]
        s0 = first[1, pl.ds(i, 1), :]
        at = pl.ds(pl.multiple_of(i * SEED, SEED), SEED)
        c1 = seed[0]
        s1 = seed[1]
        tab[at, :NF] = (c0 * c1 - s0 * s1).astype(jnp.bfloat16)
        tab[at, NF:] = (-(s0 * c1 + c0 * s1)).astype(jnp.bfloat16)
        return carry

    lax.fori_loop(0, steps, make_rows, 0)

    r_dev = live_ref.shape[1]
    lane = lax.broadcasted_iota(jnp.int32, (r_sub, r_dev), 1)
    line = lax.broadcasted_iota(jnp.int32, (r_sub, r_dev), 0) + me * r_sub
    weights = []
    for s in range(shots):
        flags = jnp.where(lane == line, live_ref[s:s + 1, :].astype(jnp.float32), 0.0)
        weights.append(jnp.sum(flags, axis=1, keepdims=True))

    def forward(s):
        weight = weights[s]
        width = 256

        def tile(n, carry):
            lanes = pl.ds(pl.multiple_of(n * width, width), width)
            lanes_im = pl.ds(pl.multiple_of(NF + n * width, width), width)
            traces = xbuf[s]
            re = jnp.dot(traces, tab[:, lanes], preferred_element_type=jnp.float32)
            im = jnp.dot(traces, tab[:, lanes_im], preferred_element_type=jnp.float32)
            c1 = rot[0:1, lanes]
            s1 = rot[1:2, lanes]
            sg = rot[2:3, lanes]
            re0, re1, re2, re3 = (re[q * rows:(q + 1) * rows] for q in range(N_Y))
            im0, im1, im2, im3 = (im[q * rows:(q + 1) * rows] for q in range(N_Y))
            x_re = re0 + sg * re2 + c1 * (re1 + re3) + s1 * (im1 - im3)
            x_im = im0 + sg * im2 + c1 * (im1 + im3) + s1 * (re3 - re1)
            obs_re = weight * x_re[:r_sub]
            obs_im = weight * x_im[:r_sub]
            syn_re = weight * x_re[r_sub:]
            syn_im = weight * x_im[r_sub:]
            spec[0, :, lanes] = obs_re
            spec[1, :, lanes] = obs_im
            spec[2, :, lanes] = syn_re
            spec[3, :, lanes] = syn_im
            sums = (
                jnp.sum(syn_re * obs_re + syn_im * obs_im, axis=0, keepdims=True),
                jnp.sum(syn_re * obs_im - syn_im * obs_re, axis=0, keepdims=True),
                jnp.sum(syn_re * syn_re + syn_im * syn_im, axis=0, keepdims=True),
            )
            for q in range(3):
                for h in range(width // 128):
                    part[s, pl.ds(q * 8 + n * (width // 128) + h, 1), :] = sums[q][:, h * 128:(h + 1) * 128]
            return carry

        lax.fori_loop(0, NF // width, tile, 0)

    def reduce(s):
        for dy, dj in SLOTS:
            py, pj = peer_of(y, j, dy, dj)
            pltpu.make_async_remote_copy(
                src_ref=part.at[s], dst_ref=from_tf.at[s, me], send_sem=tf_send.at[s], recv_sem=tf_recv.at[s],
                device_id={"tf": py * N_J + pj}, device_id_type=MESH).start()
        from_tf[s, pl.ds(me, 1)] = part[s][None]
        wait_bytes(from_tf.at[s, pl.ds(0, N_TF - 1)], tf_recv.at[s])
        sum_tf[s] = jnp.sum(from_tf[s], axis=0)
        src, done = sum_tf, from_tf
        for buf, dst, size, pos, send, recv in (
            (from_x, sum_x, n_x, x, x_send, x_recv),
            (from_z, total, n_zh, zh, z_send, z_recv),
        ):
            for d in range(1, size):
                there = zh * n_x + (x + d) % n_x if buf is from_x else ((zh + d) % n_zh) * n_x + x
                pltpu.make_async_remote_copy(
                    src_ref=src.at[s], dst_ref=buf.at[s, pos], send_sem=send.at[s], recv_sem=recv.at[s],
                    device_id={"rcv": there}, device_id_type=MESH).start()
            buf[s, pl.ds(pos, 1)] = src[s][None]
            if size > 1:
                wait_bytes(buf.at[s, pl.ds(0, size - 1)], recv.at[s])
            dst[s] = jnp.sum(buf[s], axis=0)
            src = dst

    def inverse(s):
        cross_re = total[s, 0:8, :]
        cross_im = total[s, 8:16, :]
        power = total[s, 16:24, :]
        denom = power + 0.001 * jnp.max(power)
        wrow[0:8, :] = cross_re / denom
        wrow[8:16, :] = cross_im / denom

        def block(k, carry):
            lanes = pl.ds(pl.multiple_of(k * 128, 128), 128)
            lanes_im = pl.ds(pl.multiple_of(NF + k * 128, 128), 128)
            w_re = wrow[pl.ds(k, 1), :]
            w_im = wrow[pl.ds(8 + k, 1), :]
            obs_re, obs_im, syn_re, syn_im = (spec[i, :, lanes] for i in range(4))
            re = w_re * syn_re - w_im * syn_im - obs_re
            im = w_re * syn_im + w_im * syn_re - obs_im
            c1 = rot[0:1, lanes]
            s1 = rot[1:2, lanes]
            sg = rot[2:3, lanes]
            turned = (
                (re, im),
                (c1 * re - s1 * im, s1 * re + c1 * im),
                (sg * re, sg * im),
                (c1 * re + s1 * im, c1 * im - s1 * re),
            )
            for q in range(N_Y):
                res[q * r_sub:(q + 1) * r_sub, lanes] = turned[q][0].astype(jnp.bfloat16)
                res[q * r_sub:(q + 1) * r_sub, lanes_im] = turned[q][1].astype(jnp.bfloat16)
            return carry

        lax.fori_loop(0, NF // 128, block, 0)

        for dj in (2, 3, 1, 0):
            _, pj = peer_of(y, j, 0, dj)
            cols = pl.ds(pl.multiple_of(pj * SPAN, SPAN), SPAN)
            sums = lax.dot_general(res[...], tab[cols, :], (((1,), (1,)), ((), ())),
                                   preferred_element_type=jnp.float32)
            outbuf[s, :, cols] = (2.0 * sums).astype(jnp.bfloat16)
            for dy in (2, 3, 1, 0):
                py, _ = peer_of(y, j, dy, 0)
                src = outbuf.at[s, pl.ds(pl.multiple_of(py * r_sub, r_sub), r_sub), cols]
                dst = out_ref.at[s, pl.ds(pl.multiple_of(me * r_sub, r_sub), r_sub), :]
                if dy == 0 and dj == 0:
                    pltpu.make_async_copy(src, dst, out_recv.at[s]).start()
                else:
                    pltpu.make_async_remote_copy(
                        src_ref=src, dst_ref=dst, send_sem=out_send.at[s], recv_sem=out_recv.at[s],
                        device_id={"tf": py * N_J + pj}, device_id_type=MESH).start()

    for s in range(shots):
        wait_bytes(xbuf.at[s], in_recv.at[s])
        forward(s)
        reduce(s)
        inverse(s)

    for s in range(shots):
        wait_bytes(out_ref.at[s], out_recv.at[s])
    for s in range(shots):
        sent = obs_ref.at[s, pl.ds(0, (N_TF - 1) * r_sub), :]
        wait_bytes(sent, in_send.at[s])
        wait_bytes(sent, in_send.at[s])
        wait_bytes(out_ref.at[s, pl.ds(0, (N_TF - 1) * r_sub), :], out_send.at[s])
        wait_bytes(from_tf.at[s, pl.ds(0, N_TF - 1)], tf_send.at[s])
        if n_x > 1:
            wait_bytes(from_x.at[s, pl.ds(0, n_x - 1)], x_send.at[s])
        if n_zh > 1:
            wait_bytes(from_z.at[s, pl.ds(0, n_zh - 1)], z_send.at[s])


def on_device(n_rcv, observed, synthetic, live, bins):
    shots, r_dev, _ = observed.shape
    r_sub = r_dev // N_TF
    n_x = min(4, n_rcv)
    n_zh = n_rcv // n_x

    def body(*refs):
        kernel(r_sub, n_x, n_zh, *refs)

    f32, bf16 = jnp.float32, jnp.bfloat16
    sums = (24, 128)
    dma = pltpu.SemaphoreType.DMA
    return pl.pallas_call(
        body,
        out_shape=jax.ShapeDtypeStruct(observed.shape, bf16),
        in_specs=[pl.BlockSpec(memory_space=pltpu.VMEM)] * 2 + [pl.BlockSpec(memory_space=pl.ANY)] * 2,
        out_specs=pl.BlockSpec(memory_space=pl.ANY),
        scratch_shapes=[
            pltpu.VMEM((shots, N_Y * 2 * r_sub, QUART), bf16),
            pltpu.VMEM((QUART, 2 * NF), bf16),
            pltpu.VMEM((2, SEED, NF), f32),
            pltpu.VMEM((2, QUART // SEED, NF), f32),
            pltpu.VMEM((8, NF), f32),
            pltpu.VMEM((4, r_sub, NF), f32),
            pltpu.VMEM((N_Y * r_sub, 2 * NF), bf16),
            pltpu.VMEM((shots, N_Y * r_sub, QUART), bf16),
            pltpu.VMEM((16, 128), f32),
            pltpu.VMEM((shots,) + sums, f32),
            pltpu.VMEM((shots, N_TF) + sums, f32),
            pltpu.VMEM((shots,) + sums, f32),
            pltpu.VMEM((shots, n_x) + sums, f32),
            pltpu.VMEM((shots,) + sums, f32),
            pltpu.VMEM((shots, n_zh) + sums, f32),
            pltpu.VMEM((shots,) + sums, f32),
        ] + [dma((shots,))] * 10,
        compiler_params=pltpu.CompilerParams(
            collective_id=0, has_side_effects=True, vmem_limit_bytes=48 * 2 ** 20),
    )(bins.reshape(1, NF), live, observed, synthetic)


def solution(mesh):
    n_rcv = mesh.shape["rcv"]

    def run(*args):
        return on_device(n_rcv, *args)

    in_specs = (P(None, "rcv", "tf"), P(None, "rcv", "tf"), P(None, "rcv"), P())
    out_specs = P(None, "rcv", "tf")
    return jax.shard_map(run, mesh=mesh, in_specs=in_specs, out_specs=out_specs, check_vma=False)
```

time: 467 us -> 78.6 us (0.17); the launches traced: 461 us -> 78.4 us
  matrix products: 279 us -> 0 us
  blocking collectives: 98 us -> 0 us
  Pallas kernels: 0 us -> 73.6 us
  local copies, waits for them, and re-layouts: 31.9 us -> 4.8 us
  waiting for transfers between devices: 26.2 us -> 0 us
  loops' own time: 11.6 us -> 0 us
  starting transfers between devices: 7.34 us -> 0 us
  other arithmetic: 5.86 us -> 0 us
    dot_general x32 -> x0, matrix products: 279 us -> none  [the longest x8 72.8 us: forward_block(): jnp.dot(block, sin_tab, preferred_element_type=jnp.float32)]
    psum x1 -> x0, blocking collectives: 77.9 us -> none  [on_device(): totals = lax.psum((cross_re, cross_im, power), ('rcv', 'tf'))]
    pallas_call x0 -> x1, Pallas kernels: none -> 73.6 us  [on_device(): pl.pallas_call(body, out_shape=jax.ShapeDtypeStruct(observed.shape, bf16)...]
    all_to_all x1 -> x0, waiting for transfers between devices: 26.2 us -> none  [on_device(): lax.all_to_all(stacked, 'tf', split_axis=2, concat_axis=3, tiled=True)]
    all_to_all x1 -> x0, blocking collectives: 20.1 us -> none  [on_device(): return lax.all_to_all(whole, 'tf', split_axis=2, concat_axis=1, tiled=True)]
    another operation x2 -> x0, loops' own time: 11.6 us -> none  [the longest x1 5.89 us: on_device(): lax.scan(inverse_block, jnp.int32(0), jnp.arange(n_blocks, dtype=jnp.int32))]
    dynamic_slice x16 -> x0, local copies, waits for them, and re-layouts: 10.1 us -> none  [on_device(): lax.scan(forward_block, (empty, empty), jnp.arange(n_blocks, dtype=jnp.in...]
    another operation x2 -> x0, local copies, waits for them, and re-layouts: 8.36 us -> none  [the longest x1 4.49 us: on_device(): stacked = jnp.stack([observed, synthetic])]
  transfers between devices with their start and end apart: 1 -> 0, of which waited for: 1 -> 0; matrix products, arithmetic and copies ran while one was open for 0% -> 0% of each run, Pallas kernels for 0% -> 0%
where the time goes in v1:
time: 78.6 us; the launch traced here: 78.4 us
  Pallas kernels  73.6 us (94%)
  local copies, waits for them, and re-layouts  4.8 us (6%)
    pallas_call x1, Pallas kernels, on_device(): pl.pallas_call(body, out_shape=jax.ShapeDtypeStruct(observed.shape, bf16)...  73.6 us
    unnamed x9, local copies, waits for them, and re-layouts  4.8 us

profile of v1, /device:TPU:1, one launch (start us, length us, event | category | flops | bytes accessed | tf_op | source)
XLA Modules:
  0.0 78.4 jit_solution(5680991196661205218)
XLA Ops:
  0.0 0.0 copy-start
  0.0 1.2 %copy-done = bf16[2,1024,256]{2,1,0:T(8,128)(2,1)S(1)} copy-done((bf16[2,1024,256]{2,1,0:T(8,128)(2,1)S(1)}, bf16[2,1024,256]{2,1,0:T(8,128)(2,1)}, u32[]{:S(2)}) %copy-start) | copy-done | bytes 1048600
  1.2 0.0 copy-start.1
  1.2 1.2 %copy-done.1 = bf16[2,1024,256]{2,1,0:T(8,128)(2,1)S(1)} copy-done((bf16[2,1024,256]{2,1,0:T(8,128)(2,1)S(1)}, bf16[2,1024,256]{2,1,0:T(8,128)(2,1)}, u32[]{:S(2)}) %copy-start.1) | copy-done | bytes 1048600
  2.5 0.0 copy-start.2
  2.5 0.7 copy-done.2
  3.1 0.0 copy-start.3
  3.2 0.7 copy-done.3
  3.8 73.6 %shard_map.46 = bf16[2,1024,256]{2,1,0:T(8,128)(2,1)S(1)} custom-call(s32[1,1024]{1,0:T(1,128)S(1)} %bitcast.1, s32[2,1024]{1,0:T(2,128)S(1)} %copy-done.2, bf16[2,1024,256]{2,1,0:T(8,128)(2,1)S(1)} %copy-done, bf16[2,1024,256]{2,1,0:T(8,128)(2,1)S(1)} %copy-done.1), custom_call_target="tpu_custom_call" | custom-call | tf_op jit(solution)/shard_map/pallas_call | solution.py:274
  77.4 1.0 %copy.6 = bf16[2,1024,256]{2,1,0:T(8,128)(2,1)} copy(bf16[2,1024,256]{2,1,0:T(8,128)(2,1)S(1)} %shard_map.46) | data formatting | bytes 2097152
Async XLA Ops:
  0.0 1.2 %copy-start = (bf16[2,1024,256]{2,1,0:T(8,128)(2,1)S(1)}, bf16[2,1024,256]{2,1,0:T(8,128)(2,1)}, u32[]{:S(2)}) copy-start(bf16[2,1024,256]{2,1,0:T(8,128)(2,1)} %refs_2_.1) | copy-start | bytes 3145732
  1.2 1.2 %copy-start.1 = (bf16[2,1024,256]{2,1,0:T(8,128)(2,1)S(1)}, bf16[2,1024,256]{2,1,0:T(8,128)(2,1)}, u32[]{:S(2)}) copy-start(bf16[2,1024,256]{2,1,0:T(8,128)(2,1)} %refs_3_.1) | copy-start | bytes 3145732
  2.5 0.7 copy-start.2
  3.1 0.7 copy-start.3

commit v2 on v1

v2 whole, which is shorter than its diff:
```python
import math

import jax
import jax.numpy as jnp
from jax import lax
from jax.experimental import pallas as pl
from jax.experimental.pallas import tpu as pltpu
from jax.sharding import PartitionSpec as P

NT = 4096
MESH = pl.DeviceIdType.MESH
N_TF = 16
N_Y = 4
N_J = 4
SPAN = NT // N_TF
QUART = NT // N_Y
NF = 1024
SEED = 64
SLOTS = ((2, 0), (2, 1), (2, 2), (2, 3), (3, 0), (1, 0), (3, 1), (1, 1),
         (3, 2), (1, 2), (3, 3), (1, 3), (0, 2), (0, 3), (0, 1))

BATCH = (4, 15)
ORDER = (2, 3, 1, 0)
GROUPS = ((0, 3), (3, 4))
X_STEPS = (2, 1, 3)
Z_STEPS = ((2, 0), (2, 1), (1, 1), (3, 1), (1, 0), (3, 0), (0, 1))
TILES = (3, 1, 2, 0)
UNROLL = True


def cos_sin(turns):
    k = turns & (NT - 1)
    quadrant = (k + NT // 8) // (NT // 4)
    angle = (k - quadrant * (NT // 4)).astype(jnp.float32) * (2.0 * math.pi / NT)
    sq = angle * angle
    s = angle + angle * sq * (-1 / 6 + sq * (1 / 120 + sq * (-1 / 5040 + sq * (1 / 362880))))
    c = 1.0 + sq * (-0.5 + sq * (1 / 24 + sq * (-1 / 720 + sq * (1 / 40320))))
    odd = (quadrant & 1) == 1
    cos = jnp.where(odd, s, c)
    sin = jnp.where(odd, c, s)
    turn = quadrant & 3
    cos = jnp.where((turn == 1) | (turn == 2), -cos, cos)
    sin = jnp.where(turn >= 2, -sin, sin)
    return cos, sin


def peer_of(y, j, dy, dj):
    dz, dc = dj // 2, dj % 2
    z = (j // 2 + dz) % 2
    c = (j + dc) % 2
    return (y + dy) % N_Y, z * 2 + c


def wait_bytes(view, sem):
    pltpu.make_async_copy(view, view, sem).wait()


def kernel(r_sub, n_x, n_zh, bins_hbm, live_hbm, obs_ref, syn_ref, out_ref,
           bins_ref, live_ref, xbuf, tab, seed, first, rot, spec, res, outbuf, wrow,
           acc, part, from_a, sum_a, from_x, sum_x, from_z, total,
           small, in_send, in_recv, a_send, a_recv, x_send, x_recv, z_send, z_recv, out_send, out_recv):
    me = lax.axis_index("tf")
    mr = lax.axis_index("rcv")
    y = me // N_J
    j = me % N_J
    x = mr % n_x
    zh = mr // n_x
    shots = 2
    rows = 2 * r_sub

    z_lo = j // 2
    core = j % 2
    z = zh * 2 + z_lo
    n_z = 2 * n_zh

    def stage(k):
        return (
            (part, from_a, sum_a, 2 * N_Y, y * 2 + core, a_send, a_recv),
            (sum_a, from_x, sum_x, n_x, x, x_send, x_recv),
            (sum_x, from_z, total, n_z, z, z_send, z_recv),
        )[k]

    def reduce_peers(k):
        if k == 0:
            return [{"tf": ((y + dy) % N_Y) * N_J + z_lo * 2 + (core + dc) % 2}
                    for dy, dc in ((2, 0), (2, 1), (1, 0), (3, 0), (1, 1), (3, 1), (0, 1))]
        if k == 1:
            return [{"rcv": zh * n_x + (x + d) % n_x} for d in X_STEPS if d < n_x]
        return [{"rcv": ((zh + dh) % n_zh) * n_x + x, "tf": y * N_J + ((z_lo + dl) % 2) * 2 + core}
                for dh, dl in Z_STEPS if dh < n_zh]

    flags = (pltpu.make_async_copy(bins_hbm, bins_ref, small.at[0]),
             pltpu.make_async_copy(live_hbm, live_ref, small.at[1]))
    for copy in flags:
        copy.start()

    barrier = pltpu.get_barrier_semaphore()
    count = 0
    greeted = [peer for peer, (dh, _) in zip(reduce_peers(2), Z_STEPS) if dh > 0] + reduce_peers(1)
    for peer in greeted:
        pl.semaphore_signal(barrier, inc=1, device_id=peer, device_id_type=MESH)
        count += 1
    for dy, dj in SLOTS:
        py, pj = peer_of(y, j, dy, dj)
        pl.semaphore_signal(barrier, inc=1, device_id={"tf": py * N_J + pj}, device_id_type=MESH)
        count += 1
    pl.semaphore_wait(barrier, count)

    def landing(s, a, dy):
        row = ORDER.index(dy) * rows + a * r_sub
        return xbuf.at[s, pl.ds(row, r_sub), pl.ds(pl.multiple_of(j * SPAN, SPAN), SPAN)]

    def send_in(s, slots):
        for dy, dj in slots:
            py, pj = peer_of(y, j, dy, dj)
            peer = py * N_J + pj
            for a, ref in enumerate((obs_ref, syn_ref)):
                pltpu.make_async_remote_copy(
                    src_ref=ref.at[s, pl.ds(pl.multiple_of(peer * r_sub, r_sub), r_sub), :],
                    dst_ref=landing(s, a, dy), send_sem=in_send.at[s], recv_sem=in_recv.at[s, ORDER.index(dy)],
                    device_id={"tf": peer}, device_id_type=MESH).start()

    for s in range(shots):
        for a, ref in enumerate((obs_ref, syn_ref)):
            pltpu.make_async_copy(
                ref.at[s, pl.ds(pl.multiple_of(me * r_sub, r_sub), r_sub), :],
                landing(s, a, 0), in_recv.at[s, ORDER.index(0)]).start()
    send_in(0, SLOTS)
    send_in(1, SLOTS[:BATCH[0]])
    for copy in flags:
        copy.wait()

    bins = bins_ref[...]
    times = lax.broadcasted_iota(jnp.int32, (SEED, NF), 0)
    cos, sin = cos_sin(times * bins)
    scale = NT ** (-0.5)
    seed[0] = cos * scale
    seed[1] = sin * scale
    steps = QUART // SEED
    times = lax.broadcasted_iota(jnp.int32, (steps, NF), 0) * SEED
    cos, sin = cos_sin(times * bins)
    first[0] = cos
    first[1] = sin
    for q in range(N_Y):
        turn = (bins * q) & 3
        rot[q:q + 1, :] = jnp.where(turn == 0, 1.0, jnp.where(turn == 2, -1.0, 0.0))
        rot[4 + q:5 + q, :] = jnp.where(turn == 1, 1.0, jnp.where(turn == 3, -1.0, 0.0))

    def make_rows(i, carry):
        c0 = first[0, pl.ds(i, 1), :]
        s0 = first[1, pl.ds(i, 1), :]
        at = pl.ds(pl.multiple_of(i * SEED, SEED), SEED)
        c1 = seed[0]
        s1 = seed[1]
        tab[at, :NF] = (c0 * c1 - s0 * s1).astype(jnp.bfloat16)
        tab[at, NF:] = (-(s0 * c1 + c0 * s1)).astype(jnp.bfloat16)
        return carry

    lax.fori_loop(0, steps, make_rows, 0)

    r_dev = live_ref.shape[1]
    lane = lax.broadcasted_iota(jnp.int32, (r_sub, r_dev), 1)
    line = lax.broadcasted_iota(jnp.int32, (r_sub, r_dev), 0) + me * r_sub
    weights = []
    for s in range(shots):
        flags = jnp.where(lane == line, live_ref[s:s + 1, :].astype(jnp.float32), 0.0)
        weights.append(jnp.sum(flags, axis=1, keepdims=True))

    def loop(n, body):
        if UNROLL:
            for i in range(n):
                body(i, 0)
        else:
            lax.fori_loop(0, n, body, 0)

    def forward_group(s, low, high):
        weight = weights[s]
        width = 256
        for g in range(low, high):
            wait_bytes(xbuf.at[s, g * rows:(g + 1) * rows], in_recv.at[s, g])

        def tile(n, carry):
            lanes = pl.ds(pl.multiple_of(n * width, width), width)
            lanes_im = pl.ds(pl.multiple_of(NF + n * width, width), width)
            traces = xbuf[s, low * rows:high * rows]
            re = jnp.dot(traces, tab[:, lanes], preferred_element_type=jnp.float32)
            im = jnp.dot(traces, tab[:, lanes_im], preferred_element_type=jnp.float32)
            x_re = None if low == 0 else acc[0, :, lanes]
            x_im = None if low == 0 else acc[1, :, lanes]
            for g in range(low, high):
                q = (y - ORDER[g] + N_Y) % N_Y
                c = rot[pl.ds(q, 1), lanes]
                d = rot[pl.ds(4 + q, 1), lanes]
                here = slice((g - low) * rows, (g - low + 1) * rows)
                a_re = c * re[here] + d * im[here]
                a_im = c * im[here] - d * re[here]
                x_re = a_re if x_re is None else x_re + a_re
                x_im = a_im if x_im is None else x_im + a_im
            if high < N_Y:
                acc[0, :, lanes] = x_re
                acc[1, :, lanes] = x_im
                return carry
            obs_re = weight * x_re[:r_sub]
            obs_im = weight * x_im[:r_sub]
            syn_re = weight * x_re[r_sub:]
            syn_im = weight * x_im[r_sub:]
            spec[s, 0, :, lanes] = obs_re
            spec[s, 1, :, lanes] = obs_im
            spec[s, 2, :, lanes] = syn_re
            spec[s, 3, :, lanes] = syn_im
            sums = (
                jnp.sum(syn_re * obs_re + syn_im * obs_im, axis=0, keepdims=True),
                jnp.sum(syn_re * obs_im - syn_im * obs_re, axis=0, keepdims=True),
                jnp.sum(syn_re * syn_re + syn_im * syn_im, axis=0, keepdims=True),
            )
            for q in range(3):
                for h in range(width // 128):
                    part[s, pl.ds(q * 8 + n * (width // 128) + h, 1), :] = sums[q][:, h * 128:(h + 1) * 128]
            return carry

        loop(NF // width, tile)

    def forward(s):
        for low, high in GROUPS:
            forward_group(s, low, high)

    def reduce_start(s, k):
        src, buf, _, size, pos, send, recv = stage(k)
        for peer in reduce_peers(k):
            pltpu.make_async_remote_copy(
                src_ref=src.at[s], dst_ref=buf.at[s, pos], send_sem=send.at[s], recv_sem=recv.at[s],
                device_id=peer, device_id_type=MESH).start()
        buf[s, pl.ds(pos, 1)] = src[s][None]

    def reduce_finish(s, k):
        _, buf, dst, size, _, _, recv = stage(k)
        if size > 1:
            wait_bytes(buf.at[s, pl.ds(0, size - 1)], recv.at[s])
        dst[s] = jnp.sum(buf[s], axis=0)

    def inverse(s):
        cross_re = total[s, 0:8, :]
        cross_im = total[s, 8:16, :]
        power = total[s, 16:24, :]
        denom = power + 0.001 * jnp.max(power)
        wrow[0:8, :] = cross_re / denom
        wrow[8:16, :] = cross_im / denom

        def block(k, carry):
            lanes = pl.ds(pl.multiple_of(k * 128, 128), 128)
            lanes_im = pl.ds(pl.multiple_of(NF + k * 128, 128), 128)
            w_re = wrow[pl.ds(k, 1), :]
            w_im = wrow[pl.ds(8 + k, 1), :]
            obs_re, obs_im, syn_re, syn_im = (spec[s, i, :, lanes] for i in range(4))
            re = w_re * syn_re - w_im * syn_im - obs_re
            im = w_re * syn_im + w_im * syn_re - obs_im
            for q in range(N_Y):
                c = rot[q:q + 1, lanes]
                d = rot[4 + q:5 + q, lanes]
                here = slice(q * r_sub, (q + 1) * r_sub)
                res[here, lanes] = (c * re - d * im).astype(jnp.bfloat16)
                res[here, lanes_im] = (d * re + c * im).astype(jnp.bfloat16)
            return carry

        loop(NF // 128, block)

        for dj in TILES:
            _, pj = peer_of(y, j, 0, dj)
            cols = pl.ds(pl.multiple_of(pj * SPAN, SPAN), SPAN)
            sums = lax.dot_general(res[...], tab[cols, :], (((1,), (1,)), ((), ())),
                                   preferred_element_type=jnp.float32)
            outbuf[s, :, cols] = (2.0 * sums).astype(jnp.bfloat16)
            for dy in (2, 3, 1, 0):
                py, _ = peer_of(y, j, dy, 0)
                src = outbuf.at[s, pl.ds(pl.multiple_of(py * r_sub, r_sub), r_sub), cols]
                dst = out_ref.at[s, pl.ds(pl.multiple_of(me * r_sub, r_sub), r_sub), :]
                if dy == 0 and dj == 0:
                    pltpu.make_async_copy(src, dst, out_recv.at[s]).start()
                else:
                    pltpu.make_async_remote_copy(
                        src_ref=src, dst_ref=dst, send_sem=out_send.at[s], recv_sem=out_recv.at[s],
                        device_id={"tf": py * N_J + pj}, device_id_type=MESH).start()

    forward(0)
    reduce_start(0, 0)
    send_in(1, SLOTS[BATCH[0]:BATCH[1]])
    reduce_finish(0, 0)
    reduce_start(0, 1)
    send_in(1, SLOTS[BATCH[1]:])
    reduce_finish(0, 1)
    reduce_start(0, 2)
    forward(1)
    reduce_start(1, 0)
    reduce_finish(0, 2)
    inverse(0)
    reduce_finish(1, 0)
    reduce_start(1, 1)
    reduce_finish(1, 1)
    reduce_start(1, 2)
    reduce_finish(1, 2)
    inverse(1)

    for s in range(shots):
        wait_bytes(out_ref.at[s], out_recv.at[s])
    for s in range(shots):
        sent = obs_ref.at[s, pl.ds(0, (N_TF - 1) * r_sub), :]
        wait_bytes(sent, in_send.at[s])
        wait_bytes(sent, in_send.at[s])
        wait_bytes(out_ref.at[s, pl.ds(0, (N_TF - 1) * r_sub), :], out_send.at[s])
        wait_bytes(from_a.at[s, pl.ds(0, 2 * N_Y - 1)], a_send.at[s])
        if n_x > 1:
            wait_bytes(from_x.at[s, pl.ds(0, n_x - 1)], x_send.at[s])
        wait_bytes(from_z.at[s, pl.ds(0, n_z - 1)], z_send.at[s])


def on_device(n_rcv, observed, synthetic, live, bins):
    shots, r_dev, _ = observed.shape
    r_sub = r_dev // N_TF
    n_x = min(4, n_rcv)
    n_zh = n_rcv // n_x

    def body(*refs):
        kernel(r_sub, n_x, n_zh, *refs)

    f32, bf16 = jnp.float32, jnp.bfloat16
    sums = (24, 128)
    dma = pltpu.SemaphoreType.DMA
    return pl.pallas_call(
        body,
        out_shape=jax.ShapeDtypeStruct(observed.shape, bf16),
        in_specs=[pl.BlockSpec(memory_space=pl.ANY)] * 4,
        out_specs=pl.BlockSpec(memory_space=pl.ANY),
        scratch_shapes=[
            pltpu.VMEM((1, NF), jnp.int32),
            pltpu.VMEM(live.shape, jnp.int32),
            pltpu.VMEM((shots, N_Y * 2 * r_sub, QUART), bf16),
            pltpu.VMEM((QUART, 2 * NF), bf16),
            pltpu.VMEM((2, SEED, NF), f32),
            pltpu.VMEM((2, QUART // SEED, NF), f32),
            pltpu.VMEM((8, NF), f32),
            pltpu.VMEM((shots, 4, r_sub, NF), f32),
            pltpu.VMEM((N_Y * r_sub, 2 * NF), bf16),
            pltpu.VMEM((shots, N_Y * r_sub, QUART), bf16),
            pltpu.VMEM((16, 128), f32),
            pltpu.VMEM((2, 2 * r_sub, NF), f32),
            pltpu.VMEM((shots,) + sums, f32),
            pltpu.VMEM((shots, 2 * N_Y) + sums, f32),
            pltpu.VMEM((shots,) + sums, f32),
            pltpu.VMEM((shots, n_x) + sums, f32),
            pltpu.VMEM((shots,) + sums, f32),
            pltpu.VMEM((shots, 2 * n_zh) + sums, f32),
            pltpu.VMEM((shots,) + sums, f32),
        ] + [dma((shots,))] * 2 + [dma((shots, N_Y))] + [dma((shots,))] * 8,
        compiler_params=pltpu.CompilerParams(
            collective_id=0, has_side_effects=True, vmem_limit_bytes=60 * 2 ** 20),
    )(bins.reshape(1, NF), live, observed, synthetic)


def solution(mesh):
    n_rcv = mesh.shape["rcv"]

    def run(*args):
        return on_device(n_rcv, *args)

    in_specs = (P(None, "rcv", "tf"), P(None, "rcv", "tf"), P(None, "rcv"), P())
    out_specs = P(None, "rcv", "tf")
    return jax.shard_map(run, mesh=mesh, in_specs=in_specs, out_specs=out_specs, check_vma=False)
```

time: 78.6 us -> 62.2 us (0.79)
  Pallas kernels: 73.6 us -> 59.6 us
  local copies, waits for them, and re-layouts: 4.8 us -> 2.26 us
    pallas_call x1, Pallas kernels: 73.6 us -> 59.6 us  [on_device(): pl.pallas_call(body, out_shape=jax.ShapeDtypeStruct(observed.shape, bf16)...]
    unnamed x9 -> x1, local copies, waits for them, and re-layouts: 4.8 us -> 2.26 us
where the time goes in v2:
time: 62.2 us; the launch traced here: 61.9 us
  Pallas kernels  59.6 us (96%)
  local copies, waits for them, and re-layouts  2.26 us (4%)
    pallas_call x1, Pallas kernels, on_device(): pl.pallas_call(body, out_shape=jax.ShapeDtypeStruct(observed.shape, bf16)...  59.6 us
    unnamed x1, local copies, waits for them, and re-layouts  2.26 us

profile of v2, /device:TPU:1, one launch (start us, length us, event | category | flops | bytes accessed | tf_op | source)
XLA Modules:
  0.0 61.9 jit_solution(16982577635162396066)
XLA Ops:
  0.0 59.6 %shard_map.46 = bf16[2,1024,256]{2,1,0:T(8,128)(2,1)} custom-call(s32[1,1024]{1,0:T(1,128)} %bitcast.1, s32[2,1024]{1,0:T(2,128)} %refs_1_.1, bf16[2,1024,256]{2,1,0:T(8,128)(2,1)} %refs_2_.1, bf16[2,1024,256]{2,1,0:T(8,128)(2,1)} %refs_3_.1), custom_call_target="tpu_custom_call" | custom-call | tf_op jit(solution)/shard_map/pallas_call | solution.py:328
  59.6 2.3 %copy.6 = bf16[2,1024,256]{2,1,0:T(8,128)(2,1)} copy(bf16[2,1024,256]{2,1,0:T(8,128)(2,1)} %shard_map.46) | data formatting | bytes 2097152
